TPU v7x, 256 devices: a whole 4x4x8 slice. The times are simulated.
256 devices in a mesh: cam: 8 (over z_lo, core), tile: 32 (over x, z_hi, y).
Axes of the slice: x: 4, y: 4, z: 8 (z_hi: 2, z_lo: 4; z = z_hi * 4 + z_lo), core: 2. Of those that a mesh axis runs over, the one named last changes fastest.
Arguments:
- queries: bfloat16 [8192, 256], P('tile'), as said below
- keys: bfloat16 [16384, 256], P(('cam', 'tile')), as said below
- values: bfloat16 [16384, 256], P(('cam', 'tile')), may hold values from -6 to 6
- grad_out: bfloat16 [8192, 256], P('tile'), may hold values from -6 to 6
- visible: int32 [64, 512], P('tile', 'cam'), may hold values from 0 to 1, as said below
- counts: int32 [512], P('cam'), may hold values from 2 to 32
Outputs:
- grad_queries: bfloat16 [8192, 256], P('tile')
- grad_keys: bfloat16 [16384, 256], P(('cam', 'tile'))
- grad_values: bfloat16 [16384, 256], P(('cam', 'tile'))
Inputs may be any that keep to these rules, and one draw needn't show every extreme that they name: Every tile has at least one visible block. `queries`: projected query features. `keys`: projected key features.
All inputs are finite; a program needn't handle non-finite values.
Results may differ from a plain program's by a relative error of at most 0.0052.
Values may be sent and summed in bfloat16 or wider, within the bound.
A program may use at most 128 MiB of HBM per device.

v0:
```python
import math
import jax
import jax.numpy as jnp
from jax import lax
from jax.sharding import PartitionSpec as P

H = 8


def shards(queries, keys, values, grad_out, visible, counts):
    row_count, width = queries.shape
    head_dim = width // H
    scale = 1.0 / math.sqrt(head_dim)
    key_all, value_all = (
        lax.all_gather(keys, "tile", axis=0, tiled=True),
        lax.all_gather(values, "tile", axis=0, tiled=True),
    )
    group = key_all.shape[0]
    block_count = counts.shape[0]
    block_keys = group // block_count
    slot_index = jnp.arange(group, dtype=jnp.int32) % block_keys
    key_valid = slot_index < jnp.repeat(counts, block_keys)
    tile_count = visible.shape[0]
    tile_rows = row_count // tile_count
    mask_tiles = (jnp.repeat(visible, block_keys, axis=1) == 1) & key_valid[None, :]
    per_step = 2
    step_count = tile_count // per_step
    step_rows = per_step * tile_rows
    query_blocks = queries.reshape(step_count, step_rows, H, head_dim)
    grad_blocks = grad_out.reshape(step_count, step_rows, H, head_dim)
    mask_blocks = mask_tiles.reshape(step_count, per_step, group)
    key_heads = key_all.reshape(group, H, head_dim)
    value_heads = value_all.reshape(group, H, head_dim)

    def scores_of(query_blk, key_mat):
        return (
            jnp.einsum("qhd,khd->hqk", query_blk, key_mat, preferred_element_type=jnp.float32)
            * scale
        )

    def row_mask(mask_blk):
        return jnp.repeat(mask_blk, tile_rows, axis=0)[None, :, :]

    def local_stats(inputs):
        query_blk, mask_blk = inputs
        scores = scores_of(query_blk, key_heads)
        allowed = row_mask(mask_blk)
        top = jnp.max(jnp.where(allowed, scores, -1e30), axis=-1)
        total = jnp.sum(jnp.where(allowed, jnp.exp(scores - top[..., None]), 0.0), axis=-1)
        return (top, total)

    local_top, local_total = lax.map(local_stats, (query_blocks, mask_blocks))
    global_top = lax.pmax(local_top, "cam")
    global_total = lax.psum(local_total * jnp.exp(local_top - global_top), "cam")
    lse_all = global_top + jnp.log(global_total)

    def probs_terms(query_blk, grad_blk, mask_blk, lse_blk, key_mat, value_mat):
        scores = scores_of(query_blk, key_mat)
        allowed = row_mask(mask_blk)
        probs = jnp.where(allowed, jnp.exp(scores - lse_blk[..., None]), 0.0)
        dprobs = jnp.einsum("qhd,khd->hqk", grad_blk, value_mat, preferred_element_type=jnp.float32)
        return (probs, dprobs)

    def local_delta(inputs):
        query_blk, grad_blk, mask_blk, lse_blk = inputs
        probs, dprobs = probs_terms(query_blk, grad_blk, mask_blk, lse_blk, key_heads, value_heads)
        return jnp.sum(probs * dprobs, axis=-1)

    delta_part = lax.map(local_delta, (query_blocks, grad_blocks, mask_blocks, lse_all))
    delta_all = lax.psum(delta_part, "cam")

    def rounded_terms(query_blk, grad_blk, mask_blk, lse_blk, delta_blk, key_mat, value_mat):
        probs, dprobs = probs_terms(query_blk, grad_blk, mask_blk, lse_blk, key_mat, value_mat)
        dscores = probs * (dprobs - delta_blk[..., None])
        return (probs.astype(jnp.bfloat16), dscores.astype(jnp.bfloat16))

    def query_grad_of(dscores_b):
        grad_q = (
            jnp.einsum("hqk,khd->qhd", dscores_b, key_heads, preferred_element_type=jnp.float32)
            * scale
        )
        return grad_q.reshape(step_rows, width)

    def grad_step(carry, inputs):
        query_blk, grad_blk, mask_blk, lse_blk, delta_blk = inputs
        probs_b, dscores_b = rounded_terms(
            query_blk, grad_blk, mask_blk, lse_blk, delta_blk, key_heads, value_heads
        )
        grad_k = (
            carry[0]
            + jnp.einsum("hqk,qhd->khd", dscores_b, query_blk, preferred_element_type=jnp.float32)
            * scale
        )
        grad_v = carry[1] + jnp.einsum(
            "hqk,qhd->khd", probs_b, grad_blk, preferred_element_type=jnp.float32
        )
        return ((grad_k, grad_v), query_grad_of(dscores_b))

    zero_kv = jnp.zeros((group, H, head_dim), jnp.float32)
    (grad_k, grad_v), query_parts = lax.scan(
        grad_step, (zero_kv, zero_kv), (query_blocks, grad_blocks, mask_blocks, lse_all, delta_all)
    )
    joined = jnp.concatenate((grad_k.reshape(group, width), grad_v.reshape(group, width)), axis=1)
    owned = lax.psum_scatter(joined, "tile", scatter_dimension=0, tiled=True)
    grad_queries = lax.psum(query_parts.reshape(row_count, width), "cam").astype(jnp.bfloat16)
    grad_keys = owned[:, :width].astype(jnp.bfloat16)
    grad_values = owned[:, width:].astype(jnp.bfloat16)
    return (grad_queries, grad_keys, grad_values)


def solution(mesh):
    in_specs = (
        P("tile", None),
        P(("cam", "tile"), None),
        P(("cam", "tile"), None),
        P("tile", None),
        P("tile", "cam"),
        P("cam"),
    )
    out_specs = (P("tile", None), P(("cam", "tile"), None), P(("cam", "tile"), None))
    return jax.shard_map(shards, mesh=mesh, in_specs=in_specs, out_specs=out_specs, check_vma=False)
```

profile of v0, /device:TPU:32, one launch (start us, length us, event | category | flops | bytes accessed | tf_op | source)
XLA Modules:
  0.0 469.4 jit_solution(15476085039806583543)
XLA Ops:
  7.2 0.7 all-gather.3.cloned.1.call-update
  7.9 0.7 all-gather.5.cloned.1.call-update
  8.7 0.7 broadcast_in_dim.83
  9.5 0.7 broadcast_compare_fusion
  10.3 0.1 eq.14
  10.4 1.0 copy.18
  11.4 1.0 copy.20
  12.4 81.8 %all-gather.3.cloned.1.call-done = bf16[2048,256]{1,0:T(8,128)(2,1)} async-done(((bf16[64,256]{1,0:T(8,128)(2,1)}), bf16[2048,256]{1,0:T(8,128)(2,1)}) %all-gather.3.cloned.1.call-update) | async-done | bytes 1048592 | tf_op jit(solution)/shard_map/all_gather | solution.py:15
  94.2 1.5 copy.19
  95.7 0.2 broadcast_in_dim.84
  95.9 3.3 select_reduce_fusion.1
  99.2 5.7 %copy-done = f32[8,256,2048]{2,1,0:T(8,128)} copy-done((f32[8,256,2048]{2,1,0:T(8,128)}, f32[8,256,2048]{2,1,0:T(8,128)S(1)}, u32[]{:S(2)}) %copy-start) | copy-done | bytes 16777240
  104.9 4.6 select_reduce_fusion
  109.5 11.9 %pmax.7 = f32[1,8,256]{2,1,0:T(8,128)S(1)} all-reduce(f32[1,8,256]{2,1,0:T(8,128)S(1)} %bitcast.44), channel_id=1, replica_groups=mesh['cam'=8,'tile'=32] {'cam'}, use_global_device_ids=true, to_apply=%region_1.2 | all-reduce | flops 2048 | bytes 16384 | tf_op jit(solution)/shard_map/pmax | solution.py:53
  121.4 14.3 %psum.21 = f32[1,8,256]{2,1,0:T(8,128)S(1)} all-reduce(f32[1,8,256]{2,1,0:T(8,128)S(1)} %bitcast_multiply_fusion), channel_id=1, replica_groups=mesh['cam'=8,'tile'=32] {'cam'}, use_global_device_ids=true, to_apply=%region_3.4 | all-reduce | flops 2048 | bytes 16384 | tf_op jit(solution)/shard_map/psum | solution.py:54
  135.7 9.1 %fusion.1 = f32[8,2048,32]{1,2,0:T(8,128)} fusion(bf16[256,8,32]{0,2,1:T(8,128)(2,1)S(1)} %bitcast.42, f32[8,256,2048]{2,1,0:T(8,128)} %copy-done, f32[8,256]{1,0:T(8,128)S(1)} %add_bitcast_fusion, pred[256,2048]{1,0:T(8,128)(4,1)S(1)} %bitcast.31), kind=kOutput, calls=%fused_computation.6 | convolution fusion | flops 285212672 | bytes 19537920 | tf_op jit(solution)/shard_map/while/body/eval_jaxpr/hqk,qhd->khd/dot_general | solution.py:94
  144.9 28.7 %all-gather.5.cloned.1.call-done = bf16[2048,256]{1,0:T(8,128)(2,1)} async-done(((bf16[64,256]{1,0:T(8,128)(2,1)}), bf16[2048,256]{1,0:T(8,128)(2,1)}) %all-gather.5.cloned.1.call-update) | async-done | bytes 1048592 | tf_op jit(solution)/shard_map/all_gather | solution.py:16
  173.6 1.5 copy.21
  175.1 12.6 %multiply_reduce_fusion = (f32[8,256]{1,0:T(8,128)S(1)}, f32[8,256,2048]{2,1,0:T(8,128)}) fusion(f32[8,256,2048]{2,1,0:T(8,128)} %copy-done, f32[8,256]{1,0:T(8,128)S(1)} %add_bitcast_fusion, pred[256,2048]{1,0:T(8,128)(4,1)S(1)} %bitcast.32, bf16[256,8,32]{0,2,1:T(8,128)(2,1)S(1)} %bitcast.43, bf16[2048,8,32]{0,2,1:T(8,128)(2,1)S(1)} %bitcast.37), kind=kOutput, calls=%fused_computation.1 | convolution fusion | flops 289404928 | bytes 35274752 | tf_op jit(solution)/shard_map/while/body/eval_jaxpr/qhd,khd->hqk/dot_general | solution.py:61
  187.7 12.1 %psum.22 = f32[8,256]{1,0:T(8,128)S(1)} all-reduce(f32[8,256]{1,0:T(8,128)S(1)} %get-tuple-element.60), channel_id=1, replica_groups=mesh['cam'=8,'tile'=32] {'cam'}, use_global_device_ids=true, to_apply=%region_5.6 | all-reduce | flops 2048 | bytes 16384 | tf_op jit(solution)/shard_map/psum | solution.py:70
  199.8 12.2 %multiply_convert_fusion = bf16[8,256,2048]{2,1,0:T(8,128)(2,1)S(1)} fusion(f32[8,256,2048]{2,1,0:T(8,128)} %get-tuple-element.61, f32[8,256,2048]{2,1,0:T(8,128)} %copy-done, f32[8,256]{1,0:T(8,128)S(1)} %psum.22, f32[8,256]{1,0:T(8,128)S(1)} %add_bitcast_fusion, pred[256,2048]{1,0:T(8,128)(4,1)S(1)} %bitcast.33), kind=kLoop, calls=%fused_computation | loop fusion | flops 25165824 | bytes 42483712 | tf_op jit(solution)/shard_map/while/body/eval_jaxpr/convert_element_type | solution.py:75
  212.0 3.2 copy-done.1
  215.2 1.5 convolution_multiply_fusion
  216.7 1.9 copy.23
  218.6 1.9 copy.24
  220.5 4.2 pad_maximum_fusion
  224.8 6.0 %convolution_multiply_fusion.1 = f32[8,256,32]{1,2,0:T(8,128)S(1)} fusion(bf16[8,256,2048]{2,1,0:T(8,128)(2,1)} %copy-done.1, bf16[2048,8,32]{0,2,1:T(8,128)(2,1)S(1)} %bitcast.36), kind=kOutput, calls=%fused_computation.10 | convolution fusion | flops 268500992 | bytes 9699328 | tf_op jit(solution)/shard_map/while/body/eval_jaxpr/hqk,khd->qhd/dot_general | solution.py:79
  230.8 0.1 copy.22
  230.9 33.8 %all-reduce.1 = bf16[256,256]{1,0:T(8,128)(2,1)} all-reduce(f32[256,256]{1,0:T(8,128)S(1)} %copy.22), channel_id=1, replica_groups=mesh['cam'=8,'tile'=32] {'cam'}, use_global_device_ids=true, to_apply=%region_6.7 | all-reduce | flops 65536 | bytes 393216 | tf_op jit(solution)/shard_map/psum | solution.py:105
  264.7 196.6 %reduce-scatter.2.cloned.1.call-done = f32[64,512]{1,0:T(8,128)} async-done(((f32[2048,512]{1,0:T(8,128)}), f32[64,512]{1,0:T(8,128)}) %reduce-scatter.2.cloned.1.call-update) | async-done | bytes 131088 | tf_op jit(solution)/shard_map/reduce_scatter | solution.py:104
  461.3 0.9 convert.4
  462.2 0.6 fusion.10
  (12 shorter events, 0.3 us)
Async XLA Ops:
  7.2 87.1 %all-gather.3.cloned.1.call-start = ((), (), s32[]{:S(2)}) async-start(), calls=%async_computation.1 | async-start | bytes 1081344 | tf_op jit(solution)/shard_map/all_gather | solution.py:15
  7.9 165.7 %all-gather.5.cloned.1.call-start = ((), (), s32[]{:S(2)}) async-start(), calls=%async_computation.2 | async-start | bytes 1081344 | tf_op jit(solution)/shard_map/all_gather | solution.py:16
  8.6 452.6 %reduce-scatter.2.cloned.1.call-start = ((), (), s32[]{:S(2)}) async-start(), calls=%async_computation.3 | async-start | bytes 4325376 | tf_op jit(solution)/shard_map/reduce_scatter | solution.py:104
  99.2 5.7 %copy-start = (f32[8,256,2048]{2,1,0:T(8,128)}, f32[8,256,2048]{2,1,0:T(8,128)S(1)}, u32[]{:S(2)}) copy-start(f32[8,256,2048]{2,1,0:T(8,128)S(1)} %get-tuple-element.59) | copy-start | bytes 50331652
  212.0 3.2 copy-start.1
Sparse Core Ops, SparseCore 0:
  11.4 82.7 all-gather.2
  97.6 75.8 all-gather.4
  224.9 236.3 reduce-scatter.1
where the time goes:
time: 470 us; the launch traced here: 469 us
  waiting for transfers between devices  308 us (66%)
  blocking collectives  72 us (15%)
  matrix products  32.5 us (7%)
  other arithmetic  22.7 us (5%)
  local copies, waits for them, and re-layouts  19.6 us (4%)
  between operations  13.9 us (3%)
    reduce_scatter x1, waiting for transfers between devices, shards(): owned = lax.psum_scatter(joined, 'tile', scatter_dimension=0, tiled=True)  197 us
    all_gather x1, waiting for transfers between devices, shards(): lax.all_gather(keys, 'tile', axis=0, tiled=True)  81.8 us
    psum x1, blocking collectives, shards(): lax.psum(query_parts.reshape(row_count, width), 'cam').astype(jnp.bfloat16)  33.8 us
    all_gather x1, waiting for transfers between devices, shards(): lax.all_gather(values, 'tile', axis=0, tiled=True)  28.7 us
    psum x1, blocking collectives, shards(): lax.psum(local_total * jnp.exp(local_top - global_top), 'cam')  14.3 us
    dot_general x1, matrix products, probs_terms(): jnp.einsum('qhd,khd->hqk', grad_blk, value_mat, preferred_element_type=jn...  12.6 us
    convert_element_type x1, other arithmetic, rounded_terms(): return (probs.astype(jnp.bfloat16), dscores.astype(jnp.bfloat16))  12.2 us
    psum x1, blocking collectives, shards(): delta_all = lax.psum(delta_part, 'cam')  12.1 us
  transfers between devices with their start and end apart: 3, of which 3 were waited for; matrix products, arithmetic and copies ran while one was open for 6% of the time, Pallas kernels for 0%

commit v1 on v0

--- a/solution.py
+++ b/solution.py
@@ -7,13 +7,20 @@
 H = 8
 
 
+def gather_over(block, name, dim):
+    size = lax.axis_size(name)
+    parts = jnp.stack([block for _ in range(size)])
+    parts = lax.all_to_all(parts, name, split_axis=0, concat_axis=0)
+    return jnp.concatenate(parts, axis=dim)
+
+
 def shards(queries, keys, values, grad_out, visible, counts):
     row_count, width = queries.shape
     head_dim = width // H
     scale = 1.0 / math.sqrt(head_dim)
     key_all, value_all = (
         lax.all_gather(keys, "tile", axis=0, tiled=True),
-        lax.all_gather(values, "tile", axis=0, tiled=True),
+        gather_over(values, "tile", 0),
     )
     group = key_all.shape[0]
     block_count = counts.shape[0]

time: 470 us -> 453 us (0.964)
  waiting for transfers between devices: 308 us -> 265 us
  starting transfers between devices: 0.11 us -> 13.1 us
  local copies, waits for them, and re-layouts: 19.6 us -> 28.2 us
    all_gather x1 -> x0, waiting for transfers between devices: 28.7 us -> none  [shards(): lax.all_gather(values, 'tile', axis=0, tiled=True)]
    all_to_all x0 -> x1, starting transfers between devices: none -> 13 us  [gather_over(): parts = lax.all_to_all(parts, name, split_axis=0, concat_axis=0)]
    all_gather x1, waiting for transfers between devices: 81.8 us -> 72.6 us  [shards(): lax.all_gather(keys, 'tile', axis=0, tiled=True)]
    reduce_scatter x1, waiting for transfers between devices: 197 us -> 191 us  [shards(): owned = lax.psum_scatter(joined, 'tile', scatter_dimension=0, tiled=True)]
    another operation x0 -> x2, local copies, waits for them, and re-layouts: none -> 5.24 us  [the longest x1 3.38 us: shards(): value_heads = value_all.reshape(group, H, head_dim)]
  transfers between devices with their start and end apart: 3 -> 3, of which waited for: 3 -> 2; matrix products, arithmetic and copies ran while one was open for 6% -> 7% of each run, Pallas kernels for 0% -> 0%
where the time goes in v1:
time: 453 us; the launch traced here: 450 us
  waiting for transfers between devices  265 us (58%)
  blocking collectives  74 us (16%)
  matrix products  32.5 us (7%)
  local copies, waits for them, and re-layouts  28.2 us (6%)
  other arithmetic  23.2 us (5%)
  between operations  14.2 us (3%)
  starting transfers between devices  13.1 us (3%)
    reduce_scatter x1, waiting for transfers between devices, shards(): owned = lax.psum_scatter(joined, 'tile', scatter_dimension=0, tiled=True)  191 us
    all_gather x1, waiting for transfers between devices, shards(): lax.all_gather(keys, 'tile', axis=0, tiled=True)  72.6 us
    psum x1, blocking collectives, shards(): lax.psum(query_parts.reshape(row_count, width), 'cam').astype(jnp.bfloat16)  33.9 us
    psum x1, blocking collectives, shards(): delta_all = lax.psum(delta_part, 'cam')  14.1 us
    psum x1, blocking collectives, shards(): lax.psum(local_total * jnp.exp(local_top - global_top), 'cam')  14.1 us
    all_to_all x1, starting transfers between devices, gather_over(): parts = lax.all_to_all(parts, name, split_axis=0, concat_axis=0)  13 us
    dot_general x1, matrix products, probs_terms(): jnp.einsum('qhd,khd->hqk', grad_blk, value_mat, preferred_element_type=jn...  12.6 us
    convert_element_type x1, other arithmetic, rounded_terms(): return (probs.astype(jnp.bfloat16), dscores.astype(jnp.bfloat16))  12.2 us
  transfers between devices with their start and end apart: 3, of which 2 were waited for; matrix products, arithmetic and copies ran while one was open for 7% of the time, Pallas kernels for 0%

profile of v1, /device:TPU:32, one launch (start us, length us, event | category | flops | bytes accessed | tf_op | source)
XLA Modules:
  0.0 449.9 jit_solution(843375833608808761)
XLA Ops:
  7.2 0.7 all-gather.2.cloned.1.call-update
  7.9 1.9 stack.2
  9.8 13.0 %all-to-all-start = ((bf16[32,64,256]{2,1,0:T(8,128)(2,1)}), bf16[32,64,256]{2,1,0:T(8,128)(2,1)S(1)}, u32[]{:S(2)}, u32[]{:S(2)}) async-start(bf16[32,64,256]{2,1,0:T(8,128)(2,1)} %stack.2), calls=%async_computation | async-start | bytes 2097152 | tf_op jit(solution)/shard_map/all_to_all | solution.py:13
  22.9 0.7 broadcast_in_dim.83
  23.7 0.7 broadcast_compare_fusion
  24.6 1.0 copy.25
  25.6 1.0 copy.27
  26.6 72.6 %all-gather.2.cloned.1.call-done = bf16[2048,256]{1,0:T(8,128)(2,1)} async-done(((bf16[64,256]{1,0:T(8,128)(2,1)}), bf16[2048,256]{1,0:T(8,128)(2,1)}) %all-gather.2.cloned.1.call-update) | async-done | bytes 1048592 | tf_op jit(solution)/shard_map/all_gather | solution.py:22
  99.3 1.5 copy.26
  100.8 0.2 broadcast_in_dim.84
  101.0 3.3 select_reduce_fusion.1
  104.2 5.7 %copy-done = f32[8,256,2048]{2,1,0:T(8,128)} copy-done((f32[8,256,2048]{2,1,0:T(8,128)}, f32[8,256,2048]{2,1,0:T(8,128)S(1)}, u32[]{:S(2)}) %copy-start) | copy-done | bytes 16777240
  109.9 4.6 %select_reduce_fusion = f32[8,256]{1,0:T(8,128)S(1)} fusion(f32[8,256,2048]{2,1,0:T(8,128)S(1)} %get-tuple-element.59, f32[8,256]{1,0:T(8,128)S(1)} %get-tuple-element.58, pred[256,2048]{1,0:T(8,128)(4,1)S(1)} %bitcast.31), kind=kLoop, calls=%fused_computation.3 | loop fusion | flops 16775168 | bytes 17317888 | tf_op jit(solution)/shard_map/while/body/eval_jaxpr/reduce_sum | solution.py:56
  114.5 11.9 %pmax.7 = f32[1,8,256]{2,1,0:T(8,128)S(1)} all-reduce(f32[1,8,256]{2,1,0:T(8,128)S(1)} %bitcast.44), channel_id=1, replica_groups=mesh['cam'=8,'tile'=32] {'cam'}, use_global_device_ids=true, to_apply=%region_1.2 | all-reduce | flops 2048 | bytes 16384 | tf_op jit(solution)/shard_map/pmax | solution.py:60
  126.5 14.1 %psum.21 = f32[1,8,256]{2,1,0:T(8,128)S(1)} all-reduce(f32[1,8,256]{2,1,0:T(8,128)S(1)} %bitcast_multiply_fusion), channel_id=1, replica_groups=mesh['cam'=8,'tile'=32] {'cam'}, use_global_device_ids=true, to_apply=%region_3.4 | all-reduce | flops 2048 | bytes 16384 | tf_op jit(solution)/shard_map/psum | solution.py:61
  140.6 9.1 %fusion.1 = f32[8,2048,32]{1,2,0:T(8,128)} fusion(bf16[256,8,32]{0,2,1:T(8,128)(2,1)S(1)} %bitcast.42, f32[8,256,2048]{2,1,0:T(8,128)} %copy-done, f32[8,256]{1,0:T(8,128)S(1)} %add_bitcast_fusion, pred[256,2048]{1,0:T(8,128)(4,1)S(1)} %bitcast.32), kind=kOutput, calls=%fused_computation.6 | convolution fusion | flops 285212672 | bytes 19537920 | tf_op jit(solution)/shard_map/while/body/eval_jaxpr/hqk,qhd->khd/dot_general | solution.py:101
  149.7 2.9 copy.31
  152.7 3.9 copy.28
  156.5 3.4 reshape_reshape.3
  159.9 12.6 %multiply_reduce_fusion = (f32[8,256]{1,0:T(8,128)S(1)}, f32[8,256,2048]{2,1,0:T(8,128)}) fusion(f32[8,256,2048]{2,1,0:T(8,128)} %copy-done, f32[8,256]{1,0:T(8,128)S(1)} %add_bitcast_fusion, pred[256,2048]{1,0:T(8,128)(4,1)S(1)} %bitcast.33, bf16[256,8,32]{0,2,1:T(8,128)(2,1)S(1)} %bitcast.43, bf16[2048,8,32]{0,2,1:T(8,128)(2,1)S(1)} %reshape_reshape.3), kind=kOutput, calls=%fused_computation.1 | convolution fusion | flops 289404928 | bytes 35274752 | tf_op jit(solution)/shard_map/while/body/eval_jaxpr/qhd,khd->hqk/dot_general | solution.py:68
  172.5 14.1 %psum.22 = f32[8,256]{1,0:T(8,128)S(1)} all-reduce(f32[8,256]{1,0:T(8,128)S(1)} %get-tuple-element.60), channel_id=1, replica_groups=mesh['cam'=8,'tile'=32] {'cam'}, use_global_device_ids=true, to_apply=%region_5.6 | all-reduce | flops 2048 | bytes 16384 | tf_op jit(solution)/shard_map/psum | solution.py:77
  186.7 12.2 %multiply_convert_fusion = bf16[8,256,2048]{2,1,0:T(8,128)(2,1)S(1)} fusion(f32[8,256,2048]{2,1,0:T(8,128)} %get-tuple-element.61, f32[8,256,2048]{2,1,0:T(8,128)} %copy-done, f32[8,256]{1,0:T(8,128)S(1)} %psum.22, f32[8,256]{1,0:T(8,128)S(1)} %add_bitcast_fusion, pred[256,2048]{1,0:T(8,128)(4,1)S(1)} %bitcast.34), kind=kLoop, calls=%fused_computation | loop fusion | flops 25165824 | bytes 42483712 | tf_op jit(solution)/shard_map/while/body/eval_jaxpr/convert_element_type | solution.py:82
  198.9 3.2 copy-done.1
  202.1 1.5 convolution_multiply_fusion
  203.6 1.9 copy.30
  205.5 4.8 %pad_maximum_fusion = f32[2048,512]{1,0:T(8,128)} fusion(f32[2048,256]{1,0:T(8,128)} %copy.31, f32[2048,256]{1,0:T(8,128)} %copy.30), kind=kLoop, calls=%fused_computation.8 | loop fusion | flops 1048576 | bytes 8388608 | tf_op jit(solution)/shard_map/concatenate | solution.py:110
  210.3 6.0 %convolution_multiply_fusion.1 = f32[8,256,32]{1,2,0:T(8,128)S(1)} fusion(bf16[8,256,2048]{2,1,0:T(8,128)(2,1)} %copy-done.1, bf16[2048,8,32]{0,2,1:T(8,128)(2,1)S(1)} %bitcast.37), kind=kOutput, calls=%fused_computation.10 | convolution fusion | flops 268500992 | bytes 9699328 | tf_op jit(solution)/shard_map/while/body/eval_jaxpr/hqk,khd->qhd/dot_general | solution.py:86
  216.3 0.1 copy.29
  216.4 33.9 %all-reduce.1 = bf16[256,256]{1,0:T(8,128)(2,1)} all-reduce(f32[256,256]{1,0:T(8,128)S(1)} %copy.29), channel_id=1, replica_groups=mesh['cam'=8,'tile'=32] {'cam'}, use_global_device_ids=true, to_apply=%region_6.7 | all-reduce | flops 65536 | bytes 393216 | tf_op jit(solution)/shard_map/psum | solution.py:112
  250.3 191.3 %reduce-scatter.2.cloned.1.call-done = f32[64,512]{1,0:T(8,128)} async-done(((f32[2048,512]{1,0:T(8,128)}), f32[64,512]{1,0:T(8,128)}) %reduce-scatter.2.cloned.1.call-update) | async-done | bytes 131088 | tf_op jit(solution)/shard_map/reduce_scatter | solution.py:111
  441.6 0.9 convert.4
  442.5 0.6 fusion.10
  (13 shorter events, 0.4 us)
Async XLA Ops:
  7.2 92.1 %all-gather.2.cloned.1.call-start = ((), (), s32[]{:S(2)}) async-start(), calls=%async_computation.2 | async-start | bytes 1081344 | tf_op jit(solution)/shard_map/all_gather | solution.py:22
  9.8 142.9 %all-to-all-start = ((bf16[32,64,256]{2,1,0:T(8,128)(2,1)}), bf16[32,64,256]{2,1,0:T(8,128)(2,1)S(1)}, u32[]{:S(2)}, u32[]{:S(2)}) async-start(bf16[32,64,256]{2,1,0:T(8,128)(2,1)} %stack.2), calls=%async_computation | async-start | bytes 2097152 | tf_op jit(solution)/shard_map/all_to_all | solution.py:13
  22.8 418.7 %reduce-scatter.2.cloned.1.call-start = ((), (), s32[]{:S(2)}) async-start(), calls=%async_computation.3 | async-start | bytes 4325376 | tf_op jit(solution)/shard_map/reduce_scatter | solution.py:111
  104.2 5.7 %copy-start = (f32[8,256,2048]{2,1,0:T(8,128)}, f32[8,256,2048]{2,1,0:T(8,128)S(1)}, u32[]{:S(2)}) copy-start(f32[8,256,2048]{2,1,0:T(8,128)S(1)} %get-tuple-element.59) | copy-start | bytes 50331652
  198.8 3.2 copy-start.1
Sparse Core Ops, SparseCore 0:
  11.4 87.8 all-gather.1
  210.4 231.1 reduce-scatter.1
